TPU v7x, 32 devices: a whole 2x2x4 slice. The times are simulated.
32 devices in a mesh: dp: 8 (over y, x, core), narrow: 4 (over z).
Axes of the slice: x: 2, y: 2, z: 4, core: 2. Of those that a mesh axis runs over, the one named last changes fastest.
Arguments:
- inputs: bfloat16 [16, 1152, 1024], P('dp', 'narrow'), may hold values from -6 to 6
- bucket: int32 [16], P('dp'), may hold values from 0 to 1, as said below
- attn_gain: bfloat16 [1024], P('dp'), may hold values from 0.5 to 1.5
- w_query: bfloat16 [1024, 1024], P('dp', 'narrow'), may hold values from -0.1875 to 0.1875
- w_key: bfloat16 [1024, 1024], P('dp', 'narrow'), may hold values from -0.1875 to 0.1875
- w_value: bfloat16 [1024, 1024], P('dp', 'narrow'), may hold values from -0.1875 to 0.1875
- w_out: bfloat16 [1024, 1024], P('narrow', 'dp'), may hold values from -6 to 6
- ffn_gain: bfloat16 [1024], P('dp'), may hold values from 0.5 to 1.5
- w_gate: bfloat16 [1024, 2816], P('dp', 'narrow'), may hold values from -0.1875 to 0.1875
- w_up: bfloat16 [1024, 2816], P('dp', 'narrow'), may hold values from -0.1875 to 0.1875
- w_down: bfloat16 [2816, 1024], P('narrow', 'dp'), may hold values from -0.109375 to 0.109375
- cotangent: bfloat16 [16, 1152, 1024], P('dp', 'narrow'), may hold values from -6 to 6
Outputs:
- outputs: bfloat16 [16, 1152, 1024], P('dp', 'narrow')
- input_grad: float32 [16, 1152, 1024], P('dp', 'narrow')
- attn_gain_grad: float32 [1024], P('dp')
- w_query_grad: float32 [1024, 1024], P('dp', 'narrow')
- w_key_grad: float32 [1024, 1024], P('dp', 'narrow')
- w_value_grad: float32 [1024, 1024], P('dp', 'narrow')
- w_out_grad: float32 [1024, 1024], P('narrow', 'dp')
- ffn_gain_grad: float32 [1024], P('dp')
- w_gate_grad: float32 [1024, 2816], P('dp', 'narrow')
- w_up_grad: float32 [1024, 2816], P('dp', 'narrow')
- w_down_grad: float32 [2816, 1024], P('narrow', 'dp')
Inputs may be any that keep to these rules, and one draw needn't show every extreme that they name: `bucket`: 1 marks a group holding one row of 1152 positions (448 px), 0 a group of three rows of 384 positions (224 px); both kinds occur in every draw.
All inputs are finite; a program needn't handle non-finite values.
Results may differ from a plain program's by a relative error of at most 0.017.
Values may be sent and summed in bfloat16 or wider, within the bound.
No kernel may reach another device: no remote copies, remote signals or barrier semaphores. Data moves between devices by JAX's collectives and lax.ppermute only.
A program may use at most 256 MiB of HBM per device.

v0:
```python
import math

import jax
import jax.numpy as jnp
from jax import lax
from jax.sharding import PartitionSpec as P

HEAD = 64
SHORT = 384


epsilon = 1e-06


def matmul(left, right):
    return jnp.dot(left, right, preferred_element_type=jnp.float32)


def norm_apply(stream, gain):
    return stream * lax.rsqrt(jnp.mean(stream * stream, axis=-1, keepdims=True) + epsilon) * gain


def gelu_product(gate_pre, up_pre):
    return jax.nn.gelu(gate_pre, approximate=True) * up_pre


def gather_weights(w_query, w_key, w_value, w_gate, w_up, w_out, w_down, attn_gain, ffn_gain):
    wide = (
        lax.all_gather(w_query, "narrow", axis=1, tiled=True),
        lax.all_gather(w_key, "narrow", axis=1, tiled=True),
        lax.all_gather(w_value, "narrow", axis=1, tiled=True),
        lax.all_gather(w_gate, "narrow", axis=1, tiled=True),
        lax.all_gather(w_up, "narrow", axis=1, tiled=True),
        lax.all_gather(w_out, "narrow", axis=0, tiled=True),
        lax.all_gather(w_down, "narrow", axis=0, tiled=True),
    )
    return (
        lax.all_gather(wide[0], "dp", axis=0, tiled=True),
        lax.all_gather(wide[1], "dp", axis=0, tiled=True),
        lax.all_gather(wide[2], "dp", axis=0, tiled=True),
        lax.all_gather(wide[3], "dp", axis=0, tiled=True),
        lax.all_gather(wide[4], "dp", axis=0, tiled=True),
        lax.all_gather(wide[5], "dp", axis=1, tiled=True),
        lax.all_gather(wide[6], "dp", axis=1, tiled=True),
        lax.all_gather(attn_gain, "dp", axis=0, tiled=True),
        lax.all_gather(ffn_gain, "dp", axis=0, tiled=True),
    )


def masked_scores(query_rows, key_rows, bucket_flag, query_pos, key_pos):
    score_scale = 1.0 / math.sqrt(HEAD)
    query_heads = query_rows.reshape(query_rows.shape[0], -1, HEAD)
    key_heads = key_rows.reshape(key_rows.shape[0], -1, HEAD)
    scores = (
        jnp.einsum("qhd,khd->hqk", query_heads, key_heads, preferred_element_type=jnp.float32)
        * score_scale
    )
    allowed = (bucket_flag == 1) | (query_pos[:, None] // SHORT == key_pos[None, :] // SHORT)
    return jnp.where(allowed[None], scores, -1e30)


def attend_rows(query_rows, key_rows, value_rows, bucket_flag, query_pos, key_pos):
    scores = masked_scores(query_rows, key_rows, bucket_flag, query_pos, key_pos)
    row_max = jnp.max(scores, axis=-1, keepdims=True)
    expo = jnp.exp(scores - row_max)
    row_total = jnp.sum(expo, axis=-1, keepdims=True)
    probs = (expo / row_total).astype(jnp.bfloat16)
    value_heads = value_rows.reshape(value_rows.shape[0], -1, HEAD)
    attended = jnp.einsum("hqk,khd->qhd", probs, value_heads, preferred_element_type=jnp.float32)
    log_total = (row_max + jnp.log(row_total))[..., 0]
    return (
        attended.astype(jnp.bfloat16).reshape(query_rows.shape[0], query_rows.shape[1]),
        log_total,
    )


def attend_grads(query_rows, key_rows, value_rows, d_att, log_sum, bucket_flag, query_pos, key_pos):
    score_scale = 1.0 / math.sqrt(HEAD)
    scores = masked_scores(query_rows, key_rows, bucket_flag, query_pos, key_pos)
    probs = jnp.exp(scores - log_sum[..., None])
    value_heads = value_rows.reshape(value_rows.shape[0], -1, HEAD)
    key_heads = key_rows.reshape(key_rows.shape[0], -1, HEAD)
    query_heads = query_rows.reshape(query_rows.shape[0], -1, HEAD)
    d_att_heads = d_att.reshape(d_att.shape[0], -1, HEAD)
    d_probs = jnp.einsum(
        "qhd,khd->hqk", d_att_heads, value_heads, preferred_element_type=jnp.float32
    )
    d_total = jnp.sum(probs * d_probs, axis=-1, keepdims=True)
    d_scores = (probs * (d_probs - d_total)).astype(jnp.bfloat16)
    d_query = (
        jnp.einsum("hqk,khd->qhd", d_scores, key_heads, preferred_element_type=jnp.float32)
        * score_scale
    )
    d_key = (
        jnp.einsum("hqk,qhd->khd", d_scores, query_heads, preferred_element_type=jnp.float32)
        * score_scale
    )
    d_value = jnp.einsum(
        "hqk,qhd->khd", probs.astype(jnp.bfloat16), d_att_heads, preferred_element_type=jnp.float32
    )
    return (
        d_query.reshape(query_rows.shape),
        d_key.reshape(key_rows.shape),
        d_value.reshape(value_rows.shape),
    )


def per_device(
    inputs,
    bucket,
    attn_gain,
    w_query,
    w_key,
    w_value,
    w_out,
    ffn_gain,
    w_gate,
    w_up,
    w_down,
    cotangent,
):
    bundle_count, row_count, width = inputs.shape
    span = row_count * lax.axis_size("narrow")
    all_pos = jnp.arange(span, dtype=jnp.int32)
    stream = inputs.astype(jnp.float32).reshape(bundle_count * row_count, width)

    def forward_pass():
        full = gather_weights(
            w_query, w_key, w_value, w_gate, w_up, w_out, w_down, attn_gain, ffn_gain
        )
        hidden = norm_apply(stream, full[7].astype(jnp.float32)).astype(jnp.bfloat16)
        query_rows = matmul(hidden, full[0]).astype(jnp.bfloat16)
        key_rows = matmul(hidden, full[1]).astype(jnp.bfloat16)
        value_rows = matmul(hidden, full[2]).astype(jnp.bfloat16)
        heads_width = query_rows.shape[1]
        query_three = query_rows.reshape(bundle_count, row_count, heads_width)
        key_three = key_rows.reshape(bundle_count, row_count, heads_width)
        value_three = value_rows.reshape(bundle_count, row_count, heads_width)
        query_use, key_use, value_use = (
            lax.all_to_all(query_three, "narrow", split_axis=2, concat_axis=1, tiled=True),
            lax.all_to_all(key_three, "narrow", split_axis=2, concat_axis=1, tiled=True),
            lax.all_to_all(value_three, "narrow", split_axis=2, concat_axis=1, tiled=True),
        )

        def attend_item(item):
            return attend_rows(item[0], item[1], item[2], item[3], all_pos, all_pos)

        attended_heads, log_total = lax.map(attend_item, (query_use, key_use, value_use, bucket))
        attended = lax.all_to_all(attended_heads, "narrow", split_axis=1, concat_axis=2, tiled=True)
        attended = attended.reshape(bundle_count * row_count, heads_width)
        middle = stream + matmul(attended, full[5])
        normed = norm_apply(middle, full[8].astype(jnp.float32)).astype(jnp.bfloat16)
        gate_pre = matmul(normed, full[3])
        up_pre = matmul(normed, full[4])
        inner_act = gelu_product(gate_pre, up_pre).astype(jnp.bfloat16)
        result = middle + matmul(inner_act, full[6])
        kept = (
            full,
            hidden,
            query_use,
            key_use,
            value_use,
            attended,
            log_total,
            middle,
            normed,
            gate_pre,
            up_pre,
            inner_act,
        )
        return (result, kept)

    result, first_kept = forward_pass()
    outputs = result.astype(jnp.bfloat16).reshape(bundle_count, row_count, width)
    second_result, kept = forward_pass()
    (
        full,
        hidden,
        query_use,
        key_use,
        value_use,
        attended,
        log_total,
        middle,
        normed,
        gate_pre,
        up_pre,
        inner_act,
    ) = kept
    gain_attn = full[7].astype(jnp.float32)
    gain_ffn = full[8].astype(jnp.float32)
    d_stream = cotangent.astype(jnp.float32).reshape(bundle_count * row_count, width)
    d_out = d_stream.astype(jnp.bfloat16)
    grad_down = jnp.einsum("rf,rd->fd", inner_act, d_out, preferred_element_type=jnp.float32)
    d_inner = jnp.einsum("rd,fd->rf", d_out, full[6], preferred_element_type=jnp.float32)
    unused_value, gelu_pull = jax.vjp(gelu_product, gate_pre, up_pre)
    d_gate_f, d_up_f = gelu_pull(d_inner)
    d_gate = d_gate_f.astype(jnp.bfloat16)
    d_up = d_up_f.astype(jnp.bfloat16)
    grad_gate = jnp.einsum("rd,rf->df", normed, d_gate, preferred_element_type=jnp.float32)
    grad_up = jnp.einsum("rd,rf->df", normed, d_up, preferred_element_type=jnp.float32)
    d_normed = jnp.einsum(
        "rf,df->rd", d_gate, full[3], preferred_element_type=jnp.float32
    ) + jnp.einsum("rf,df->rd", d_up, full[4], preferred_element_type=jnp.float32)
    unused_norm, norm_pull_ffn = jax.vjp(norm_apply, middle, gain_ffn)
    d_middle_norm, grad_ffn_gain = norm_pull_ffn(d_normed)
    d_middle = d_stream + d_middle_norm
    d_branch = d_middle.astype(jnp.bfloat16)
    grad_out = jnp.einsum("rh,rd->hd", attended, d_branch, preferred_element_type=jnp.float32)
    d_attended = jnp.einsum(
        "rd,hd->rh", d_branch, full[5], preferred_element_type=jnp.float32
    ).astype(jnp.bfloat16)
    heads_width = d_attended.shape[1]
    d_att_three = d_attended.reshape(bundle_count, row_count, heads_width)
    d_att_heads = lax.all_to_all(d_att_three, "narrow", split_axis=2, concat_axis=1, tiled=True)

    def grads_item(item):
        d_q, d_k, d_v = attend_grads(
            item[0], item[1], item[2], item[3], item[4], item[5], all_pos, all_pos
        )
        return (d_q.astype(jnp.bfloat16), d_k.astype(jnp.bfloat16), d_v.astype(jnp.bfloat16))

    d_query_h, d_key_h, d_value_h = lax.map(
        grads_item, (query_use, key_use, value_use, d_att_heads, log_total, bucket)
    )
    d_query_r, d_key_r, d_value_r = (
        lax.all_to_all(d_query_h, "narrow", split_axis=1, concat_axis=2, tiled=True),
        lax.all_to_all(d_key_h, "narrow", split_axis=1, concat_axis=2, tiled=True),
        lax.all_to_all(d_value_h, "narrow", split_axis=1, concat_axis=2, tiled=True),
    )
    d_query = d_query_r.reshape(bundle_count * row_count, heads_width)
    d_key = d_key_r.reshape(bundle_count * row_count, heads_width)
    d_value = d_value_r.reshape(bundle_count * row_count, heads_width)
    grad_query = jnp.einsum("rd,rh->dh", hidden, d_query, preferred_element_type=jnp.float32)
    grad_key = jnp.einsum("rd,rh->dh", hidden, d_key, preferred_element_type=jnp.float32)
    grad_value = jnp.einsum("rd,rh->dh", hidden, d_value, preferred_element_type=jnp.float32)
    d_hidden = jnp.einsum("rh,dh->rd", d_query, full[0], preferred_element_type=jnp.float32)
    d_hidden = d_hidden + jnp.einsum(
        "rh,dh->rd", d_key, full[1], preferred_element_type=jnp.float32
    )
    d_hidden = d_hidden + jnp.einsum(
        "rh,dh->rd", d_value, full[2], preferred_element_type=jnp.float32
    )
    unused_attn, norm_pull_attn = jax.vjp(norm_apply, stream, gain_attn)
    d_stream_norm, grad_attn_gain = norm_pull_attn(d_hidden)
    input_grad = (d_middle + d_stream_norm).reshape(bundle_count, row_count, width)
    gain_attn_total, gain_ffn_total = lax.psum((grad_attn_gain, grad_ffn_gain), "narrow")
    summed = (
        lax.psum_scatter(grad_query, "dp", scatter_dimension=0, tiled=True),
        lax.psum_scatter(grad_key, "dp", scatter_dimension=0, tiled=True),
        lax.psum_scatter(grad_value, "dp", scatter_dimension=0, tiled=True),
        lax.psum_scatter(grad_gate, "dp", scatter_dimension=0, tiled=True),
        lax.psum_scatter(grad_up, "dp", scatter_dimension=0, tiled=True),
        lax.psum_scatter(grad_out, "dp", scatter_dimension=1, tiled=True),
        lax.psum_scatter(grad_down, "dp", scatter_dimension=1, tiled=True),
        lax.psum_scatter(gain_attn_total, "dp", scatter_dimension=0, tiled=True),
        lax.psum_scatter(gain_ffn_total, "dp", scatter_dimension=0, tiled=True),
    )
    mats = (
        lax.psum_scatter(
            summed[0].astype(jnp.bfloat16), "narrow", scatter_dimension=1, tiled=True
        ).astype(jnp.float32),
        lax.psum_scatter(
            summed[1].astype(jnp.bfloat16), "narrow", scatter_dimension=1, tiled=True
        ).astype(jnp.float32),
        lax.psum_scatter(
            summed[2].astype(jnp.bfloat16), "narrow", scatter_dimension=1, tiled=True
        ).astype(jnp.float32),
        lax.psum_scatter(
            summed[3].astype(jnp.bfloat16), "narrow", scatter_dimension=1, tiled=True
        ).astype(jnp.float32),
        lax.psum_scatter(
            summed[4].astype(jnp.bfloat16), "narrow", scatter_dimension=1, tiled=True
        ).astype(jnp.float32),
        lax.psum_scatter(
            summed[5].astype(jnp.bfloat16), "narrow", scatter_dimension=0, tiled=True
        ).astype(jnp.float32),
        lax.psum_scatter(
            summed[6].astype(jnp.bfloat16), "narrow", scatter_dimension=0, tiled=True
        ).astype(jnp.float32),
    )
    gains = (summed[7], summed[8])
    return (
        outputs,
        input_grad,
        gains[0],
        mats[0],
        mats[1],
        mats[2],
        mats[5],
        gains[1],
        mats[3],
        mats[4],
        mats[6],
    )


def solution(mesh):
    placed = (
        P("dp", "narrow", None),
        P("dp"),
        P("dp"),
        P("dp", "narrow"),
        P("dp", "narrow"),
        P("dp", "narrow"),
        P("narrow", "dp"),
        P("dp"),
        P("dp", "narrow"),
        P("dp", "narrow"),
        P("narrow", "dp"),
        P("dp", "narrow", None),
    )
    return jax.shard_map(
        per_device,
        mesh=mesh,
        in_specs=placed,
        out_specs=(
            P("dp", "narrow", None),
            P("dp", "narrow", None),
            P("dp"),
            P("dp", "narrow"),
            P("dp", "narrow"),
            P("dp", "narrow"),
            P("narrow", "dp"),
            P("dp"),
            P("dp", "narrow"),
            P("dp", "narrow"),
            P("narrow", "dp"),
        ),
        check_vma=False,
    )
```

profile of v0, /device:TPU:0, one launch (start us, length us, event | category | flops | bytes accessed | tf_op | source)
XLA Modules:
  0.0 1261.9 jit_solution(17955432609905019882)
XLA Ops:
  7.2 17.6 %all_gather.69 = bf16[128,1024]{1,0:T(8,128)(2,1)} all-gather(bf16[128,256]{1,0:T(8,128)(2,1)} %param.22), channel_id=1, replica_groups=mesh['dp'=8,'narrow'=4] {'narrow'}, dimensions={1}, use_global_device_ids=true | all-gather | bytes 327680 | tf_op jit(solution)/shard_map/all_gather | solution.py:30
  71.2 18.1 %all_gather.74 = bf16[128,2816]{0,1:T(8,128)(2,1)} all-gather(bf16[128,704]{0,1:T(8,128)(2,1)S(1)} %copy-done.43), channel_id=1, replica_groups=mesh['dp'=8,'narrow'=4] {'narrow'}, dimensions={1}, use_global_device_ids=true | all-gather | bytes 901120 | tf_op jit(solution)/shard_map/all_gather | solution.py:32
  89.3 16.1 %all_gather.76 = bf16[128,2816]{0,1:T(8,128)(2,1)} all-gather(bf16[128,704]{0,1:T(8,128)(2,1)S(1)} %copy-done.44), channel_id=1, replica_groups=mesh['dp'=8,'narrow'=4] {'narrow'}, dimensions={1}, use_global_device_ids=true | all-gather | bytes 901120 | tf_op jit(solution)/shard_map/all_gather | solution.py:33
  134.9 28.8 %all-to-all-done.2 = bf16[2,288,1024]{1,0,2:T(2,128)(2,1)S(1)} async-done(((bf16[2,288,1024]{1,0,2:T(2,128)(2,1)}), bf16[2,288,1024]{1,0,2:T(2,128)(2,1)S(1)}, u32[]{:S(2)}, u32[]{:S(2)}) %all-to-all-start.2) | async-done | bytes 1179680 | tf_op jit(solution)/shard_map/all_to_all | solution.py:141
  177.2 27.0 %all-to-all-done.1 = bf16[2,288,1024]{1,0,2:T(2,128)(2,1)S(1)} async-done(((bf16[2,288,1024]{1,0,2:T(2,128)(2,1)}), bf16[2,288,1024]{1,0,2:T(2,128)(2,1)S(1)}, u32[]{:S(2)}, u32[]{:S(2)}) %all-to-all-start.1) | async-done | bytes 1179680 | tf_op jit(solution)/shard_map/all_to_all | solution.py:140
  208.6 49.8 %all_gather.78 = bf16[2816,128]{1,0:T(8,128)(2,1)} all-gather(bf16[704,128]{1,0:T(8,128)(2,1)S(1)} %copy-done.45), channel_id=1, replica_groups=mesh['dp'=8,'narrow'=4] {'narrow'}, dimensions={0}, use_global_device_ids=true | all-gather | bytes 901120 | tf_op jit(solution)/shard_map/all_gather | solution.py:35
  285.0 73.0 %while.49 = (s32[]{:T(128)}, bf16[2,1152,256]{1,2,0:T(8,128)(2,1)}, f32[2,4,1152]{2,1,0:T(4,128)}, bf16[2,1152,256]{1,2,0:T(8,128)(2,1)}, s32[2]{0:T(128)S(1)}, ...) while((s32[]{:T(128)}, bf16[2,1152,256]{1,2,0:T(8,128)(2,1)}, ...), condition=%wide.region_9.10_spmd.clone, body=%wide.region_6.9_spmd.clone.sunk | while | flops 1404380160 | bytes 170777456 | solution.py:148
  376.1 16.1 %all-to-all-done.4 = bf16[2,1152,256]{2,0,1:T(2,128)(2,1)} async-done(((bf16[2,1152,256]{2,0,1:T(2,128)(2,1)}), bf16[2,1152,256]{2,0,1:T(2,128)(2,1)}, u32[]{:S(2)}, u32[]{:S(2)}) %all-to-all-start.4) | async-done | bytes 1179680 | tf_op jit(solution)/shard_map/all_to_all | solution.py:149
  465.6 29.9 %all-to-all-done.5 = bf16[2,288,1024]{1,0,2:T(2,128)(2,1)} async-done(((bf16[2,288,1024]{1,0,2:T(2,128)(2,1)}), bf16[2,288,1024]{1,0,2:T(2,128)(2,1)}, u32[]{:S(2)}, u32[]{:S(2)}) %all-to-all-start.5) | async-done | bytes 1179680 | tf_op jit(solution)/shard_map/all_to_all | solution.py:215
  506.3 117.6 %while.50 = (s32[]{:T(128)}, bf16[2,1152,256]{1,2,0:T(8,128)(2,1)}, bf16[2,1152,256]{1,2,0:T(8,128)(2,1)}, bf16[2,1152,256]{1,2,0:T(8,128)(2,1)}, bf16[2,1152,25...) while((s32[]{:T(128)}, bf16[2,1152,256]{1,2,0:T(8,128)(2,1)}, ...), condition=%wide.region_14.15_spmd.clone, body=%wide.region_12.14_spmd.clone.sunk | while | flops 3449304576 | bytes 278807680 | solution.py:223
  635.1 25.4 %all-to-all-done.8 = bf16[2,1152,256]{2,0,1:T(2,128)(2,1)} async-done(((bf16[2,1152,256]{2,0,1:T(2,128)(2,1)}), bf16[2,1152,256]{2,0,1:T(2,128)(2,1)}, u32[]{:S(2)}, u32[]{:S(2)}) %all-to-all-start.8) | async-done | bytes 1179680 | tf_op jit(solution)/shard_map/all_to_all | solution.py:229
  672.4 31.6 %all_to_all.162 = bf16[2,1152,256]{2,0,1:T(2,128)(2,1)S(1)} all-to-all(bf16[2,1152,256]{2,0,1:T(2,128)(2,1)} %copy.128), channel_id=1, replica_groups=mesh['dp'=8,'narrow'=4] {'narrow'}, dimensions={1} | all-to-all | bytes 2359296 | tf_op jit(solution)/shard_map/all_to_all | solution.py:228
  714.4 31.1 %all_to_all.163 = bf16[2,1152,256]{2,0,1:T(2,128)(2,1)S(1)} all-to-all(bf16[2,1152,256]{2,0,1:T(2,128)(2,1)} %copy.125), channel_id=1, replica_groups=mesh['dp'=8,'narrow'=4] {'narrow'}, dimensions={1} | all-to-all | bytes 2359296 | tf_op jit(solution)/shard_map/all_to_all | solution.py:227
  793.4 58.4 %while.48 = (s32[]{:T(128)}, bf16[2,1152,256]{1,2,0:T(8,128)(2,1)}, bf16[2,1152,256]{1,2,0:T(8,128)(2,1)}, s32[2]{0:T(128)S(1)}, bf16[2,1152,256]{1,2,0:T(8,128)...) while((s32[]{:T(128)}, bf16[2,1152,256]{1,2,0:T(8,128)(2,1)}, ...), condition=%wide.region_4.5_spmd.clone, body=%wide.region_1.4_spmd.clone.sunk | while | flops 2089177344 | bytes 12298879 | solution.py:148
  866.7 21.2 %all-to-all-done.3 = bf16[2,1152,256]{2,0,1:T(2,128)(2,1)S(1)} async-done(((bf16[2,1152,256]{2,0,1:T(2,128)(2,1)}), bf16[2,1152,256]{2,0,1:T(2,128)(2,1)S(1)}, u32[]{:S(2)}, u32[]{:S(2)}) %all-to-all-start.3) | async-done | bytes 1179680 | tf_op jit(solution)/shard_map/all_to_all | solution.py:149
  889.2 28.4 %reduce-scatter.37.cloned.1.call-done = f32[128,2816]{1,0:T(8,128)} async-done(((f32[1024,2816]{1,0:T(8,128)}), f32[128,2816]{1,0:T(8,128)}) %reduce-scatter.37.cloned.1.call-update) | async-done | bytes 1441808 | tf_op jit(solution)/shard_map/reduce_scatter | solution.py:253
  934.3 73.7 %reduce-scatter.35.cloned.1.call-done = f32[128,2816]{1,0:T(8,128)} async-done(((f32[1024,2816]{1,0:T(8,128)}), f32[128,2816]{1,0:T(8,128)}) %reduce-scatter.35.cloned.1.call-update) | async-done | bytes 1441808 | tf_op jit(solution)/shard_map/reduce_scatter | solution.py:252
  1010.6 16.5 %add_convert_fusion = bf16[576,1024]{1,0:T(8,128)(2,1)} fusion(f32[576,1024]{1,0:T(8,128)} %copy-done.62, bf16[2816,1024]{1,0:T(8,128)(2,1)} %all-gather.22.cloned.1.call-done, f32[576,2816]{1,0:T(8,128)} %fusion.87, bf16[1024,2816]{0,1:T(8,128)(2,1)} %all-gather.20.cloned.1.call-done, f32[1024]{0:T(1024)S(1)} %bitcast.304, f32[576]{0:T(1024)S(1)} %add_rsqrt_fusion), kind=kOutput, calls=%fused_computation.125 | convolution fusion | flops 6662946816 | bytes 21567744 | tf_op jit(solution)/shard_map/dot_general | solution.py:16
  1032.0 66.1 %reduce-scatter.39.cloned.1.call-done = f32[2816,128]{1,0:T(8,128)} async-done(((f32[2816,1024]{1,0:T(8,128)}), f32[2816,128]{1,0:T(8,128)}) %reduce-scatter.39.cloned.1.call-update) | async-done | bytes 1441808 | tf_op jit(solution)/shard_map/reduce_scatter | solution.py:255
  1143.0 18.1 %reduce-scatter.25.cloned.1.call-done = bf16[128,256]{1,0:T(8,128)(2,1)} async-done(((bf16[128,1024]{1,0:T(8,128)(2,1)}), bf16[128,256]{1,0:T(8,128)(2,1)}) %reduce-scatter.25.cloned.1.call-update) | async-done | bytes 65552 | tf_op jit(solution)/shard_map/reduce_scatter | solution.py:263
  1162.6 19.3 %reduce-scatter.21.cloned.1.call-done = bf16[128,256]{1,0:T(8,128)(2,1)} async-done(((bf16[128,1024]{1,0:T(8,128)(2,1)}), bf16[128,256]{1,0:T(8,128)(2,1)}) %reduce-scatter.21.cloned.1.call-update) | async-done | bytes 65552 | tf_op jit(solution)/shard_map/reduce_scatter | solution.py:260
  1183.4 21.8 %reduce-scatter.45.cloned.1.call-done = bf16[704,128]{1,0:T(8,128)(2,1)} async-done(((bf16[2816,128]{1,0:T(8,128)(2,1)}), bf16[704,128]{1,0:T(8,128)(2,1)}) %reduce-scatter.45.cloned.1.call-update) | async-done | bytes 180240
  1207.2 21.9 %reduce-scatter.43.cloned.1.call-done = bf16[704,128]{1,0:T(8,128)(2,1)} async-done(((bf16[2816,128]{1,0:T(8,128)(2,1)}), bf16[704,128]{1,0:T(8,128)(2,1)}) %reduce-scatter.43.cloned.1.call-update) | async-done | bytes 180240
  1231.0 22.2 %reduce-scatter.41.cloned.1.call-done = bf16[704,128]{1,0:T(8,128)(2,1)} async-done(((bf16[2816,128]{1,0:T(8,128)(2,1)}), bf16[704,128]{1,0:T(8,128)(2,1)}) %reduce-scatter.41.cloned.1.call-update) | async-done | bytes 180240 | tf_op jit(solution)/shard_map/reduce_scatter | solution.py:278
  (431 shorter events, 639.6 us)
Async XLA Ops:
  7.2 108.9 %all-gather.14.cloned.1.call-start = ((), (), s32[]{:S(2)}) async-start(), calls=%async_computation.25 | async-start | bytes 2359296 | tf_op jit(solution)/shard_map/all_gather | solution.py:39
  24.9 101.2 %all-gather.12.cloned.1.call-start = ((), (), s32[]{:S(2)}) async-start(), calls=%async_computation.24 | async-start | bytes 2359296 | tf_op jit(solution)/shard_map/all_gather | solution.py:38
  39.9 127.4 %all-gather.10.cloned.1.call-start = ((), (), s32[]{:S(2)}) async-start(), calls=%async_computation.23 | async-start | bytes 2359296 | tf_op jit(solution)/shard_map/all_gather | solution.py:40
  55.4 340.4 %all-gather.16.cloned.1.call-start = ((), (), s32[]{:S(2)}) async-start(), calls=%async_computation.26 | async-start | bytes 2359296 | tf_op jit(solution)/shard_map/all_gather | solution.py:43
  71.1 331.2 %all-gather.18.cloned.1.call-start = ((), (), s32[]{:S(2)}) async-start(), calls=%async_computation.27 | async-start | bytes 6488064 | tf_op jit(solution)/shard_map/all_gather | solution.py:41
  89.3 322.2 %all-gather.20.cloned.1.call-start = ((), (), s32[]{:S(2)}) async-start(), calls=%async_computation.28 | async-start | bytes 6488064 | tf_op jit(solution)/shard_map/all_gather | solution.py:42
  122.5 41.3 %all-to-all-start.2 = ((bf16[2,288,1024]{1,0,2:T(2,128)(2,1)}), bf16[2,288,1024]{1,0,2:T(2,128)(2,1)S(1)}, u32[]{:S(2)}, u32[]{:S(2)}) async-start(bf16[2,288,1024]{1,0,2:T(2,128)(2,1)} %copy.103), calls=%async_computation.2 | async-start | bytes 3145728 | tf_op jit(solution)/shard_map/all_to_all | solution.py:141
  163.7 40.5 %all-to-all-start.1 = ((bf16[2,288,1024]{1,0,2:T(2,128)(2,1)}), bf16[2,288,1024]{1,0,2:T(2,128)(2,1)S(1)}, u32[]{:S(2)}, u32[]{:S(2)}) async-start(bf16[2,288,1024]{1,0,2:T(2,128)(2,1)} %copy.100), calls=%async_computation.1 | async-start | bytes 3145728 | tf_op jit(solution)/shard_map/all_to_all | solution.py:140
  204.2 69.7 %all-to-all-start = ((bf16[2,288,1024]{1,0,2:T(2,128)(2,1)}), bf16[2,288,1024]{1,0,2:T(2,128)(2,1)}, u32[]{:S(2)}, u32[]{:S(2)}) async-start(bf16[2,288,1024]{1,0,2:T(2,128)(2,1)} %copy.97), calls=%async_computation | async-start | bytes 3145728 | tf_op jit(solution)/shard_map/all_to_all | solution.py:142
  208.6 212.3 %all-gather.22.cloned.1.call-start = ((), (), s32[]{:S(2)}) async-start(), calls=%async_computation.29 | async-start | bytes 6488064 | tf_op jit(solution)/shard_map/all_gather | solution.py:44
  459.7 330.8 %reduce-scatter.31.cloned.1.call-start = ((), (), s32[]{:S(2)}) async-start(), calls=%async_computation.36 | async-start | bytes 4718592 | tf_op jit(solution)/shard_map/reduce_scatter | solution.py:254
  632.4 227.4 %reduce-scatter.27.cloned.1.call-start = ((), (), s32[]{:S(2)}) async-start(), calls=%async_computation.34 | async-start | bytes 4718592 | tf_op jit(solution)/shard_map/reduce_scatter | solution.py:251
  668.1 193.6 %reduce-scatter.23.cloned.1.call-start = ((), (), s32[]{:S(2)}) async-start(), calls=%async_computation.32 | async-start | bytes 4718592 | tf_op jit(solution)/shard_map/reduce_scatter | solution.py:250
  710.1 153.4 %reduce-scatter.19.cloned.1.call-start = ((), (), s32[]{:S(2)}) async-start(), calls=%async_computation.30 | async-start | bytes 4718592 | tf_op jit(solution)/shard_map/reduce_scatter | solution.py:249
  751.9 165.7 %reduce-scatter.37.cloned.1.call-start = ((), (), s32[]{:S(2)}) async-start(), calls=%async_computation.39 | async-start | bytes 12976128 | tf_op jit(solution)/shard_map/reduce_scatter | solution.py:253
  763.4 244.6 %reduce-scatter.35.cloned.1.call-start = ((), (), s32[]{:S(2)}) async-start(), calls=%async_computation.38 | async-start | bytes 12976128 | tf_op jit(solution)/shard_map/reduce_scatter | solution.py:252
  774.7 323.4 %reduce-scatter.39.cloned.1.call-start = ((), (), s32[]{:S(2)}) async-start(), calls=%async_computation.40 | async-start | bytes 12976128 | tf_op jit(solution)/shard_map/reduce_scatter | solution.py:255
  790.4 349.7 %reduce-scatter.33.cloned.1.call-start = ((), (), s32[]{:S(2)}) async-start(), calls=%async_computation.37 | async-start | bytes 327680 | tf_op jit(solution)/shard_map/reduce_scatter | solution.py:275
  859.7 281.8 %reduce-scatter.29.cloned.1.call-start = ((), (), s32[]{:S(2)}) async-start(), calls=%async_computation.35 | async-start | bytes 327680 | tf_op jit(solution)/shard_map/reduce_scatter | solution.py:266
  861.6 299.5 %reduce-scatter.25.cloned.1.call-start = ((), (), s32[]{:S(2)}) async-start(), calls=%async_computation.33 | async-start | bytes 327680 | tf_op jit(solution)/shard_map/reduce_scatter | solution.py:263
  863.5 318.4 %reduce-scatter.21.cloned.1.call-start = ((), (), s32[]{:S(2)}) async-start(), calls=%async_computation.31 | async-start | bytes 327680 | tf_op jit(solution)/shard_map/reduce_scatter | solution.py:260
  865.4 339.9 %reduce-scatter.45.cloned.1.call-start = ((), (), s32[]{:S(2)}) async-start(), calls=%async_computation.43 | async-start | bytes 901120
  920.2 308.9 %reduce-scatter.43.cloned.1.call-start = ((), (), s32[]{:S(2)}) async-start(), calls=%async_computation.42 | async-start | bytes 901120
  1010.6 242.6 %reduce-scatter.41.cloned.1.call-start = ((), (), s32[]{:S(2)}) async-start(), calls=%async_computation.41 | async-start | bytes 901120 | tf_op jit(solution)/shard_map/reduce_scatter | solution.py:278
  (93 other events, 1055.9 us)
Sparse Core Ops, SparseCore 0:
  25.0 27.9 all-gather.13
  54.9 27.8 all-gather.11
  84.7 27.8 all-gather.9
  114.3 28.1 all-gather.15
  144.3 44.3 all-gather.17
  190.4 44.3 all-gather.19
  258.5 44.5 all-gather.21
  465.7 51.7 reduce-scatter.30
  668.2 49.4 reduce-scatter.26
  721.0 51.3 reduce-scatter.22
  776.1 51.3 reduce-scatter.18
  830.8 86.7 reduce-scatter.36
  921.1 86.7 reduce-scatter.34
  1011.3 86.7 reduce-scatter.38
  1100.2 19.6 reduce-scatter.32
  1122.7 17.8 reduce-scatter.28
  1143.3 17.7 reduce-scatter.24
  1163.9 17.9 reduce-scatter.20
  1184.2 20.9 reduce-scatter.44
  1207.4 21.6 reduce-scatter.42
  1231.4 21.7 reduce-scatter.40
where the time goes:
time: 1270 us; the launch traced here: 1260 us
  waiting for transfers between devices  420 us (33%)
  matrix products  303 us (24%)
  blocking collectives  254 us (20%)
  local copies, waits for them, and re-layouts  157 us (12%)
  other arithmetic  75.5 us (6%)
  starting transfers between devices  29.7 us (2%)
  between operations  16 us (1%)
    reduce_scatter x1, waiting for transfers between devices, per_device(): lax.psum_scatter(grad_gate, 'dp', scatter_dimension=0, tiled=True)  73.7 us
    reduce_scatter x1, waiting for transfers between devices, per_device(): lax.psum_scatter(grad_down, 'dp', scatter_dimension=1, tiled=True)  66.1 us
    dot_general x9, matrix products, matmul(): return jnp.dot(left, right, preferred_element_type=jnp.float32)  63.9 us
    all_gather x1, blocking collectives, gather_weights(): lax.all_gather(w_down, 'narrow', axis=0, tiled=True)  49.8 us
    dot_general x4, matrix products, attend_rows(): jnp.einsum('hqk,khd->qhd', probs, value_heads, preferred_element_type=jnp...  45.7 us
    unnamed x23, waiting for transfers between devices  44.1 us
    dot_general x4, matrix products, masked_scores(): jnp.einsum('qhd,khd->hqk', query_heads, key_heads, preferred_element_type...  37.3 us
    all_to_all x2, waiting for transfers between devices, forward_pass(): lax.all_to_all(attended_heads, 'narrow', split_axis=1, concat_axis=2, til...  37.3 us
  transfers between devices with their start and end apart: 28, of which 14 were waited for; matrix products, arithmetic and copies ran while one was open for 37% of the time, Pallas kernels for 0%

commit v1 on v0

v1 whole, which is shorter than its diff:
```python
import functools

import jax
import jax.numpy as jnp
from jax import lax
from jax.experimental import pallas as pl
from jax.experimental.pallas import tpu as pltpu
from jax.sharding import PartitionSpec as P

HEAD = 64
SHORT = 384
EPS = 1e-06
BLOCKS = 4
f32 = jnp.float32
bf16 = jnp.bfloat16


def dot_nn(left, right):
    return jnp.dot(left, right, preferred_element_type=f32)


def dot_nt(left, right):
    return lax.dot_general(left, right, (((1,), (1,)), ((), ())), preferred_element_type=f32)


def call(kernel, grid, prefetch, in_specs, out_specs, out_shape, scratch, flops, moved, vmem):
    return pl.pallas_call(
        kernel,
        grid_spec=pltpu.PrefetchScalarGridSpec(
            num_scalar_prefetch=prefetch,
            grid=grid,
            in_specs=in_specs,
            out_specs=out_specs,
            scratch_shapes=scratch,
        ),
        out_shape=out_shape,
        compiler_params=pltpu.CompilerParams(vmem_limit_bytes=vmem << 20),
        cost_estimate=pl.CostEstimate(flops=flops, bytes_accessed=moved, transcendentals=0),
    )


def shaped(shape, dtype):
    return jax.ShapeDtypeStruct(shape, dtype)


def rms_of(rows):
    return lax.rsqrt(jnp.mean(rows * rows, axis=-1, keepdims=True) + EPS)


def qkv_kernel(me_ref, x_ref, gain_ref, w_ref, hidden_ref, q_ref, k_ref, v_ref):
    rows = x_ref[...].astype(f32)
    hidden_ref[...] = (rows * rms_of(rows) * gain_ref[...]).astype(bf16)
    wide = w_ref.shape[3]
    half = w_ref.shape[1] * 128
    for part, ref in enumerate((q_ref, k_ref, v_ref)):
        total = None
        for step in range(BLOCKS):
            start = pl.multiple_of((me_ref[0] ^ step) * wide, wide)
            weight = w_ref[step, :, part * 128 : (part + 1) * 128, :].reshape(half, wide)
            piece = dot_nt(hidden_ref[:, pl.ds(start, wide)], weight)
            total = piece if total is None else total + piece
        if part == 0:
            total = total * (HEAD**-0.5)
        ref[...] = total.astype(bf16)


def qkv_call(me, rows, gain, weights):
    count, width = rows.shape
    half = weights.shape[1] * 128
    tile = count // 4
    row_spec = pl.BlockSpec((tile, width), lambda i, me: (i, 0))
    half_spec = pl.BlockSpec((tile, half), lambda i, me: (i, 0))
    return call(
        qkv_kernel,
        (count // tile,),
        1,
        [
            row_spec,
            pl.BlockSpec((1, width), lambda i, me: (0, 0)),
            pl.BlockSpec(weights.shape, lambda i, me: (0, 0, 0, 0)),
        ],
        [row_spec, half_spec, half_spec, half_spec],
        [shaped(rows.shape, bf16)] + [shaped((count, half), bf16)] * 3,
        [],
        2 * count * width * half * 3,
        12 << 20,
        40,
    )(me, rows, gain, weights)


def two_heads(rows):
    low = lax.broadcasted_iota(jnp.int32, rows.shape, 1) < HEAD
    zero = jnp.zeros_like(rows)
    return jnp.concatenate([jnp.where(low, rows, zero), jnp.where(low, zero, rows)], axis=0)


def one_pair(both):
    half = both.shape[1] // 2
    return jnp.concatenate([both[:HEAD, :half], both[HEAD:, half:]], axis=0)


def attend_kernel(flag_ref, q_ref, k_ref, v_ref, out_ref, probs_ref, v_turned):
    block = pl.program_id(1)

    @pl.when(block == 0)
    def _():
        v_turned[...] = v_ref[...].T

    queries = two_heads(q_ref[...])

    def attend(keys, values):
        scores = dot_nt(keys, queries)
        expo = jnp.exp(scores - jnp.max(scores, axis=0, keepdims=True))
        probs = (expo * (1.0 / jnp.sum(expo, axis=0, keepdims=True))).astype(bf16)
        probs_ref[0, 0, : keys.shape[0], :] = probs
        out_ref[...] = one_pair(dot_nn(values, probs)).T.astype(bf16)

    @pl.when(flag_ref[0] == 1)
    def _():
        attend(k_ref[...], v_turned[...])

    @pl.when(flag_ref[0] != 1)
    def _():
        start = pl.multiple_of(block * SHORT, SHORT)
        attend(k_ref[pl.ds(start, SHORT), :], v_turned[:, pl.ds(start, SHORT)])


def attend_call(flag, q, k, v):
    count, half = q.shape
    pairs, blocks = half // 128, count // SHORT
    some = pl.BlockSpec((SHORT, 128), lambda j, i, flag: (i, j))
    every = pl.BlockSpec((count, 128), lambda j, i, flag: (0, j))
    return call(
        attend_kernel,
        (pairs, blocks),
        1,
        [some, every, every],
        [some, pl.BlockSpec((1, 1, count, 2 * SHORT), lambda j, i, flag: (j, i, 0, 0))],
        [shaped(q.shape, bf16), shaped((pairs, blocks, count, 2 * SHORT), bf16)],
        [pltpu.VMEM((128, count), bf16)],
        4 * 4 * count * count * half,
        28 << 20,
        48,
    )(flag, q, k, v)


def branch_kernel(me_ref, att_ref, w_ref, out_ref):
    wide = w_ref.shape[3]
    for step in range(BLOCKS):
        start = pl.multiple_of((me_ref[0] ^ step) * wide, wide)
        weight = w_ref[step].reshape(att_ref.shape[1], wide)
        out_ref[:, pl.ds(start, wide)] = dot_nn(att_ref[...], weight).astype(bf16)


def branch_call(me, attended, weights):
    count, half = attended.shape
    width = weights.shape[0] * weights.shape[3]
    tile = count // 4
    block = weights.shape[:2] + (128,) + weights.shape[3:]
    return call(
        branch_kernel,
        (count // tile,),
        1,
        [
            pl.BlockSpec((tile, half), lambda i, me: (i, 0)),
            pl.BlockSpec(block, lambda i, me: (0, 0, 3, 0)),
        ],
        pl.BlockSpec((tile, width), lambda i, me: (i, 0)),
        shaped((count, width), bf16),
        [],
        2 * count * width * half,
        5 << 20,
        24,
    )(me, attended, weights)


def middle_kernel(x_ref, one_ref, two_ref, gain_ref, middle_ref, normed_ref):
    middle = x_ref[...].astype(f32) + (one_ref[...].astype(f32) + two_ref[...].astype(f32))
    middle_ref[...] = middle
    normed_ref[...] = (middle * rms_of(middle) * gain_ref[...]).astype(bf16)


def middle_call(rows, one, two, gain):
    count, width = rows.shape
    tile = count // 4
    spec = pl.BlockSpec((tile, width), lambda i: (i, 0))
    return call(
        middle_kernel,
        (count // tile,),
        0,
        [spec, spec, spec, pl.BlockSpec((1, width), lambda i: (0, 0))],
        [spec, spec],
        [shaped(rows.shape, f32), shaped(rows.shape, bf16)],
        [],
        0,
        14 << 20,
        32,
    )(rows, one, two, gain)


def ffn_kernel(
    normed_ref, d_out_ref, w_ref, result_ref, d_normed_ref, grads_ref, result, d_normed, inner_t, gate_t, up_t
):
    chunk, chunks = pl.program_id(0), pl.num_programs(0)
    parts, pieces, kinds, depth, wide = w_ref.shape
    units = pieces * depth
    tile = SHORT

    def weight(step, kind):
        return w_ref[step, :, kind].reshape(units, wide)

    def columns(step):
        return slice(step * wide, (step + 1) * wide)

    def rows_step(index, carry):
        rows = pl.ds(pl.multiple_of(index * tile, tile), tile)

        def project(ref, kind):
            total = None
            for step in range(parts):
                piece = dot_nt(ref[rows, columns(step)], weight(step, kind))
                total = piece if total is None else total + piece
            return total

        gate, up, d_inner = project(normed_ref, 0), project(normed_ref, 1), project(d_out_ref, 2)
        square = gate * gate
        bent = jnp.tanh(0.7978845608 * gate * (1.0 + 0.044715 * square))
        half = 0.5 * (1.0 + bent)
        gelu = gate * half
        slope = half + 0.5 * gate * (1.0 - bent * bent) * (
            0.7978845608 * (1.0 + 3 * 0.044715 * square)
        )
        inner = (gelu * up).astype(bf16)
        d_gate = (d_inner * up * slope).astype(bf16)
        d_up = (d_inner * gelu).astype(bf16)
        inner_t[:, rows] = inner.T
        gate_t[:, rows] = d_gate.T
        up_t[:, rows] = d_up.T
        for step in range(parts):
            forward = dot_nn(inner, weight(step, 2))
            backward = dot_nn(d_gate, weight(step, 0)) + dot_nn(d_up, weight(step, 1))

            @pl.when(chunk == 0)
            def _():
                result[rows, columns(step)] = forward
                d_normed[rows, columns(step)] = backward

            @pl.when(chunk > 0)
            def _():
                result[rows, columns(step)] += forward
                d_normed[rows, columns(step)] += backward

        return carry

    lax.fori_loop(0, normed_ref.shape[0] // tile, rows_step, 0)
    for step in range(parts):
        block = (pieces, depth, wide)
        here = normed_ref[:, columns(step)]
        grads_ref[step, :, 0] = dot_nn(gate_t[...], here).reshape(block).astype(bf16)
        grads_ref[step, :, 1] = dot_nn(up_t[...], here).reshape(block).astype(bf16)
        there = d_out_ref[:, columns(step)]
        grads_ref[step, :, 2] = dot_nn(inner_t[...], there).reshape(block).astype(bf16)

    @pl.when(chunk == chunks - 1)
    def _():
        result_ref[...] = result[...].astype(bf16)
        d_normed_ref[...] = d_normed[...].astype(bf16)


def ffn_call(normed, d_out, weights):
    count, width = normed.shape
    parts, pieces, kinds, depth, wide = weights.shape
    chunks = 2
    part = depth // chunks
    units = pieces * part
    whole = pl.BlockSpec((count, width), lambda f: (0, 0))
    weight_spec = pl.BlockSpec((parts, pieces, kinds, part, wide), lambda f: (0, 0, 0, f, 0))
    return call(
        ffn_kernel,
        (chunks,),
        0,
        [whole, whole, weight_spec],
        [whole, whole, weight_spec],
        [shaped(normed.shape, bf16), shaped(normed.shape, bf16), shaped(weights.shape, bf16)],
        [pltpu.VMEM((count, width), f32)] * 2 + [pltpu.VMEM((units, count), bf16)] * 3,
        18 * count * width * pieces * depth,
        28 << 20,
        60,
    )(normed, d_out, weights)


def turn_kernel(
    me_ref, middle_ref, one_ref, two_ref, cot_ref, gain_ref, w_ref, d_middle_ref, d_branch_ref, d_att_ref, gain_grad_ref
):
    middle = middle_ref[...]
    rms = rms_of(middle)
    scaled = middle * rms
    d_normed = one_ref[...].astype(f32) + two_ref[...].astype(f32)
    pulled = d_normed * gain_ref[...]
    d_middle = cot_ref[...].astype(f32) + rms * (
        pulled - scaled * jnp.mean(pulled * scaled, axis=-1, keepdims=True)
    )
    d_middle_ref[...] = d_middle
    d_branch_ref[...] = d_middle.astype(bf16)

    @pl.when(pl.program_id(0) == 0)
    def _():
        gain_grad_ref[...] = jnp.zeros_like(gain_grad_ref)

    gain_grad_ref[...] += jnp.sum(d_normed * scaled, axis=0, keepdims=True)
    wide = w_ref.shape[3]
    total = None
    for step in range(BLOCKS):
        start = pl.multiple_of((me_ref[0] ^ step) * wide, wide)
        piece = dot_nt(d_branch_ref[:, pl.ds(start, wide)], w_ref[step].reshape(d_att_ref.shape[1], wide))
        total = piece if total is None else total + piece
    d_att_ref[...] = total.astype(bf16)


def turn_call(me, middle, one, two, cot, gain, weights):
    count, width = middle.shape
    half = weights.shape[1] * 128
    tile = count // 4
    spec = pl.BlockSpec((tile, width), lambda i, me: (i, 0))
    line = pl.BlockSpec((1, width), lambda i, me: (0, 0))
    block = weights.shape[:2] + (128,) + weights.shape[3:]
    return call(
        turn_kernel,
        (count // tile,),
        1,
        [spec, spec, spec, spec, line, pl.BlockSpec(block, lambda i, me: (0, 0, 3, 0))],
        [spec, spec, pl.BlockSpec((tile, half), lambda i, me: (i, 0)), line],
        [
            shaped(middle.shape, f32),
            shaped(middle.shape, bf16),
            shaped((count, half), bf16),
            shaped((1, width), f32),
        ],
        [],
        2 * count * width * half,
        22 << 20,
        40,
    )(me, middle, one, two, cot, gain, weights)


def attend_back_kernel(
    flag_ref, q_ref, k_ref, v_ref, out_ref, d_out_ref, probs_ref, dq_ref, dk_ref, dv_ref, k_turned, dk_sum, dv_sum
):
    block, blocks = pl.program_id(1), pl.num_programs(1)

    @pl.when(block == 0)
    def _():
        k_turned[...] = k_ref[...].T

    queries, grads = two_heads(q_ref[...]), two_heads(d_out_ref[...])
    turned = (d_out_ref[...].astype(f32) * out_ref[...].astype(f32)).T
    delta = jnp.concatenate(
        [
            jnp.sum(turned[:HEAD], axis=0, keepdims=True),
            jnp.sum(turned[HEAD:], axis=0, keepdims=True),
        ],
        axis=1,
    )

    def back(values, keys_turned):
        probs = probs_ref[0, 0, : values.shape[0], :]
        d_probs = dot_nt(values, grads)
        d_scores = (probs.astype(f32) * (d_probs - delta)).astype(bf16)
        d_query = one_pair(dot_nn(keys_turned, d_scores)).T * (HEAD**-0.5)
        dq_ref[...] = d_query.astype(bf16)
        return dot_nn(d_scores, queries), dot_nn(probs, grads)

    @pl.when(flag_ref[0] == 1)
    def _():
        d_key, d_value = back(v_ref[...], k_turned[...])

        @pl.when(block == 0)
        def _():
            dk_sum[...] = d_key
            dv_sum[...] = d_value

        @pl.when(block > 0)
        def _():
            dk_sum[...] += d_key
            dv_sum[...] += d_value

    @pl.when(flag_ref[0] != 1)
    def _():
        rows = pl.ds(pl.multiple_of(block * SHORT, SHORT), SHORT)
        d_key, d_value = back(v_ref[rows, :], k_turned[:, rows])
        dk_sum[rows, :] = d_key
        dv_sum[rows, :] = d_value

    @pl.when(block == blocks - 1)
    def _():
        dk_ref[...] = dk_sum[...].astype(bf16)
        dv_ref[...] = dv_sum[...].astype(bf16)


def attend_back_call(flag, q, k, v, out, d_out, probs):
    count, half = q.shape
    pairs, blocks = half // 128, count // SHORT
    some = pl.BlockSpec((SHORT, 128), lambda j, i, flag: (i, j))
    every = pl.BlockSpec((count, 128), lambda j, i, flag: (0, j))
    return call(
        attend_back_kernel,
        (pairs, blocks),
        1,
        [
            some,
            every,
            every,
            some,
            some,
            pl.BlockSpec((1, 1, count, 2 * SHORT), lambda j, i, flag: (j, i, 0, 0)),
        ],
        [some, every, every],
        [shaped(q.shape, bf16)] * 3,
        [pltpu.VMEM((128, count), bf16)] + [pltpu.VMEM((count, 128), f32)] * 2,
        4 * 8 * count * count * half,
        30 << 20,
        48,
    )(flag, q, k, v, out, d_out, probs)


def square_kernel(
    me_ref, dq_ref, dk_ref, dv_ref, att_ref, hidden_ref, d_branch_ref, w_ref, d_hidden_ref, grads_ref, turned
):
    lefts = (dq_ref, dk_ref, dv_ref, att_ref)

    @pl.when(pl.program_id(0) == 0)
    def _():
        for part, ref in enumerate(lefts):
            turned[part] = ref[...].T

    pieces, wide = w_ref.shape[1], w_ref.shape[3]
    total = None
    for part, ref in enumerate(lefts):
        rows = slice(part * 128, (part + 1) * 128)
        right = d_branch_ref if part == 3 else hidden_ref
        grad = dot_nn(turned[part], right[...])
        grads_ref[0, :, rows, :] = grad.reshape(pieces, 128, wide).astype(bf16)
        if part < 3:
            piece = dot_nn(ref[...], w_ref[0, :, rows, :].reshape(pieces * 128, wide))
            total = piece if total is None else total + piece
    d_hidden_ref[...] = total.astype(bf16)


def square_call(me, dq, dk, dv, attended, hidden, d_branch, weights):
    count, half = dq.shape
    width = hidden.shape[1]
    parts, pieces, depth, wide = weights.shape
    every = pl.BlockSpec((count, half), lambda d, me: (0, 0))
    column = pl.BlockSpec((count, wide), lambda d, me: (0, me[0] ^ d))
    return call(
        square_kernel,
        (parts,),
        1,
        [every] * 4
        + [column, column, pl.BlockSpec((1, pieces, depth, wide), lambda d, me: (d, 0, 0, 0))],
        [column, pl.BlockSpec((1, pieces, depth, wide), lambda d, me: (me[0] ^ d, 0, 0, 0))],
        [shaped(hidden.shape, bf16), shaped(weights.shape, bf16)],
        [pltpu.VMEM((4, half, count), bf16)],
        14 * count * width * half,
        24 << 20,
        40,
    )(me, dq, dk, dv, attended, hidden, d_branch, weights)


def output_kernel(core_ref, middle_ref, own_ref, other_ref, out_ref):
    out_ref[0] = (
        middle_ref[0, 0] + (own_ref[0, 0].astype(f32) + other_ref[0].astype(f32))
    ).astype(bf16)


def output_call(core, middle, own, other):
    slots, halves, tile, width = own.shape
    mine = pl.BlockSpec((1, 1, tile, width), lambda i, core: (i, core[0], 0, 0))
    plain = pl.BlockSpec((1, tile, width), lambda i, core: (i, 0, 0))
    return call(
        output_kernel,
        (slots,),
        1,
        [mine, mine, plain],
        plain,
        shaped((slots, tile, width), bf16),
        [],
        0,
        6 << 20,
        16,
    )(core, middle.reshape(own.shape), own, other)


def input_kernel(core_ref, x_ref, d_middle_ref, own_ref, other_ref, gain_ref, out_ref, gain_grad_ref):
    rows = x_ref[0, 0].astype(f32)
    rms = rms_of(rows)
    scaled = rows * rms
    d_hidden = own_ref[0, 0].astype(f32) + other_ref[0].astype(f32)
    pulled = d_hidden * gain_ref[...]
    out_ref[0] = (
        d_middle_ref[0, 0]
        + rms * (pulled - scaled * jnp.mean(pulled * scaled, axis=-1, keepdims=True))
    ).astype(bf16)

    @pl.when(pl.program_id(0) == 0)
    def _():
        gain_grad_ref[...] = jnp.zeros_like(gain_grad_ref)

    gain_grad_ref[...] += jnp.sum(d_hidden * scaled, axis=0, keepdims=True)


def input_call(core, rows, d_middle, own, other, gain):
    slots, halves, tile, width = own.shape
    mine = pl.BlockSpec((1, 1, tile, width), lambda i, core: (i, core[0], 0, 0))
    plain = pl.BlockSpec((1, tile, width), lambda i, core: (i, 0, 0))
    line = pl.BlockSpec((1, width), lambda i, core: (0, 0))
    return call(
        input_kernel,
        (slots,),
        1,
        [mine, mine, mine, plain, line],
        [plain, line],
        [shaped((slots, tile, width), bf16), shaped((1, width), f32)],
        [],
        0,
        8 << 20,
        16,
    )(core, rows.reshape(own.shape), d_middle.reshape(own.shape), own, other, gain)


def per_device(
    inputs,
    bucket,
    attn_gain,
    w_query,
    w_key,
    w_value,
    w_out,
    ffn_gain,
    w_gate,
    w_up,
    w_down,
    cotangent,
):
    dp, narrow = lax.axis_size("dp"), lax.axis_size("narrow")
    chips = dp // 2
    core, chip = lax.axis_index("dp") % 2, lax.axis_index("dp") // 2
    place = lax.axis_index("narrow")
    same_core = [[2 * m + c for m in range(chips)] for c in range(2)]
    by_core = core == 0
    bundle, row_count, width = inputs.shape
    tile = row_count // 2
    own_width = w_query.shape[0]

    def to_core(value):
        return lax.ppermute(value, "dp", [(i, i ^ 1) for i in range(dp)])

    def along(value, shift):
        return lax.ppermute(
            value, "narrow", [(i, (i + shift) % narrow) for i in range(narrow)]
        )

    def to_chip(value, flip):
        return lax.ppermute(value, "dp", [(i, i ^ (2 * flip)) for i in range(dp)])

    def ordered(mine, theirs, axis):
        join = functools.partial(jnp.concatenate, axis=axis)
        return jnp.where(by_core, join([mine, theirs]), join([theirs, mine]))

    def pick(value, index, axis):
        return lax.dynamic_index_in_dim(value, index, axis, keepdims=False)

    def across(value):
        moved = [pick(value, place, 0)] + [
            along(pick(value, (place + k) % narrow, 0), k) for k in range(1, narrow)
        ]
        stacked = jnp.stack(moved)
        order = (place - jnp.arange(narrow)) % narrow
        return jnp.stack([pick(stacked, order[i], 0) for i in range(narrow)])

    def group_in(value):
        halves = value.reshape(bundle, 2, tile, width)
        theirs = to_core(pick(halves, 1 - core, 1))
        groups = ordered(pick(halves, core, 1), theirs, 0)
        mine = across(groups)
        other = to_core(mine)
        return ordered(mine[:, None], other[:, None], 1).reshape(-1, width)

    def group_out(value):
        groups = across(value).reshape(2, bundle, tile, width)
        theirs = to_core(pick(groups, 1 - core, 0))
        mine = pick(groups, core, 0)
        return ordered(mine[:, None], theirs[:, None], 1).reshape(bundle, row_count, width)

    def halves_of(*parts):
        both = jnp.concatenate(
            [part.reshape(2, part.shape[0] // 2, own_width) for part in parts], axis=1
        )
        return ordered(pick(both, core, 0), to_core(pick(both, 1 - core, 0)), 1)

    square = halves_of(w_query.T, w_key.T, w_value.T, w_out)
    ffn = halves_of(w_gate.T, w_up.T, w_down)
    gains = ordered(*(lambda g: (g, to_core(g)))(jnp.stack([attn_gain, ffn_gain])), 1)

    def canonical(value):
        if chips == BLOCKS:
            return value
        parts = value.reshape((BLOCKS, chips // BLOCKS) + value.shape[1:])
        return jnp.moveaxis(parts, 1, -2).reshape(
            (BLOCKS,) + value.shape[1:-1] + (width // BLOCKS,)
        )

    def scattered(value):
        if chips == BLOCKS:
            return value
        parts = value.reshape(
            value.shape[:-1] + (chips // BLOCKS, width // chips)
        )
        return jnp.moveaxis(parts, -2, 1).reshape(
            (chips,) + value.shape[1:-1] + (width // chips,)
        )

    stacked = jnp.stack([square] + [along(square, k) for k in range(1, narrow)])
    x_rows = group_in(inputs)
    if chips == 4:
        first, second = to_chip(stacked, 1), to_chip(stacked, 2)
        third = jnp.concatenate(
            [to_chip(first[: narrow // 2], 2), to_chip(second[narrow // 2 :], 1)]
        )
        square_full = jnp.stack([stacked, first, second, third])
        me = chip.astype(jnp.int32)[None]
        gain_first, gain_second = to_chip(gains, 1), to_chip(gains, 2)
        relative = jnp.stack([gains, gain_first, gain_second, to_chip(gain_first, 2)])
        full_gains = jnp.stack([pick(relative, chip ^ d, 0) for d in range(4)], axis=1)
    else:
        gathered = lax.all_gather(stacked, "dp", axis_index_groups=same_core)
        square_full = canonical(gathered)
        me = jnp.zeros((1,), jnp.int32)
        full_gains = jnp.moveaxis(
            lax.all_gather(gains, "dp", axis_index_groups=same_core), 0, 1
        )
    full_gains = full_gains.reshape(2, 1, width).astype(f32)

    everyone = [
        [(2 * m + c) * narrow + j for m in range(chips) for j in range(narrow)] for c in range(2)
    ]
    gathered = lax.all_gather(ffn, ("dp", "narrow"), axis_index_groups=everyone)
    ffn_full = canonical(gathered.reshape(chips, narrow, ffn.shape[0], ffn.shape[1]))
    ffn_full = ffn_full.reshape(BLOCKS, narrow, 3, ffn.shape[0] // 3, width // BLOCKS)
    cot_rows = group_in(cotangent)

    flags = ordered(bucket, lax.ppermute(bucket.astype(f32), "dp", [(i, i ^ 1) for i in range(dp)]).astype(jnp.int32), 0)
    flag = pick(flags, place, 0)[None]
    core_index = core.astype(jnp.int32)[None]

    hidden, q, k, v = qkv_call(me, x_rows, full_gains[0], square_full)
    attended, probs = attend_call(flag, q, k, v)
    branch = branch_call(me, attended, square_full)
    middle, normed = middle_call(x_rows, branch, to_core(branch), full_gains[1])
    result, d_normed, ffn_grads = ffn_call(normed, cot_rows, ffn_full)

    d_middle, d_branch, d_att, ffn_gain_grad = turn_call(
        me, middle, d_normed, to_core(d_normed), cot_rows, full_gains[1], square_full
    )

    def reduce_chips(value):
        value = scattered(value)
        flat = value.reshape(-1, value.shape[-1])
        got = lax.psum_scatter(
            flat, "dp", scatter_dimension=0, tiled=True, axis_index_groups=same_core
        )
        return got.reshape(value.shape[1:])

    ffn_part = reduce_chips(ffn_grads.reshape(BLOCKS, narrow, ffn.shape[0], width // BLOCKS))

    by_rows = (narrow, 2, tile, width)
    result = result.reshape(by_rows)
    result_other = to_core(pick(result, 1 - core, 1))
    outputs = group_out(output_call(core_index, middle, result, result_other))

    dq, dk, dv = attend_back_call(flag, q, k, v, attended, d_att, probs)
    d_hidden, square_grads = square_call(
        me, dq, dk, dv, attended, hidden, d_branch, square_full
    )
    d_hidden = d_hidden.reshape(by_rows)
    d_hidden_other = to_core(pick(d_hidden, 1 - core, 1))
    input_rows, attn_gain_grad = input_call(
        core_index, x_rows, d_middle, d_hidden, d_hidden_other, full_gains[0]
    )
    input_grad = group_out(input_rows).astype(f32)

    square_part = reduce_chips(square_grads)

    gain_line = jnp.concatenate([attn_gain_grad, 0.5 * ffn_gain_grad], axis=0)
    gain_sum = lax.psum(gain_line, ("dp", "narrow"))
    gain_own = lax.dynamic_slice_in_dim(
        gain_sum, lax.axis_index("dp") * own_width, own_width, axis=1
    )

    def finish(mine, received):
        total = mine.astype(f32)
        for piece in received:
            total = total + piece.astype(f32)
        both = total.reshape(total.shape[0], 2, own_width)
        keep = pick(both, core, 1)
        theirs = to_core(pick(both, 1 - core, 1).astype(bf16)).astype(f32)
        return jnp.where(by_core, jnp.stack([keep, theirs]), jnp.stack([theirs, keep]))

    square_done = finish(
        square_part[0], [along(square_part[k], -k) for k in range(1, narrow)]
    )
    ffn_done = finish(
        pick(ffn_part, place, 0),
        [along(pick(ffn_part, (place + k) % narrow, 0), k) for k in range(1, narrow)],
    )

    def unpack(done, parts):
        size = done.shape[1] // parts
        return [
            done[:, i * size : (i + 1) * size].reshape(2 * size, own_width) for i in range(parts)
        ]

    g_query, g_key, g_value, g_out = unpack(square_done, 4)
    g_gate, g_up, g_down = unpack(ffn_done, 3)
    return (
        outputs,
        input_grad,
        gain_own[0],
        g_query.T,
        g_key.T,
        g_value.T,
        g_out,
        gain_own[1],
        g_gate.T,
        g_up.T,
        g_down,
    )


def solution(mesh):
    rows = P("dp", "narrow", None)
    tall, flat = P("dp", "narrow"), P("narrow", "dp")
    return jax.shard_map(
        per_device,
        mesh=mesh,
        in_specs=(rows, P("dp"), P("dp"), tall, tall, tall, flat, P("dp"), tall, tall, flat, rows),
        out_specs=(rows, rows, P("dp"), tall, tall, tall, flat, P("dp"), tall, tall, flat),
        check_vma=False,
    )
```

time: 1270 us -> 546 us (0.43)
  matrix products: 303 us -> 0 us
  blocking collectives: 254 us -> 49.9 us
  waiting for transfers between devices: 420 us -> 237 us
  Pallas kernels: 0 us -> 125 us
  local copies, waits for them, and re-layouts: 157 us -> 38.6 us
  other arithmetic: 75.5 us -> 17 us
  starting transfers between devices: 29.7 us -> 55.2 us
    dot_general x39 -> x0, matrix products: 283 us -> none  [the longest x9 63.9 us: matmul(): return jnp.dot(left, right, preferred_element_type=jnp.float32)]
    ppermute x0 -> x44, waiting for transfers between devices: none -> 217 us  [the longest x21 182 us: along(): lax.ppermute(value, 'narrow', [(i, (i + shift) % narrow) for i in range(n...]
    reduce_scatter x12 -> x2, waiting for transfers between devices: 228 us -> 19.6 us  [reduce_chips(): lax.psum_scatter(flat, 'dp', scatter_dimension=0, tiled=True, axis_index_...]
    all_gather x9 -> x0, blocking collectives: 165 us -> none  [the longest x1 49.8 us: gather_weights(): lax.all_gather(w_down, 'narrow', axis=0, tiled=True)]
    all_to_all x7 -> x0, waiting for transfers between devices: 148 us -> none  [the longest x2 37.3 us: forward_pass(): lax.all_to_all(attended_heads, 'narrow', split_axis=1, concat_axis=2, til...]
    pallas_call x0 -> x10, Pallas kernels: none -> 125 us  [the longest x1 58.1 us: ffn_call(): call(ffn_kernel, (chunks,), 0, [whole, whole, weight_spec], [whole, whole...]
    all_to_all x2 -> x0, blocking collectives: 62.7 us -> none  [the longest x1 31.6 us: per_device(): lax.all_to_all(d_key_h, 'narrow', split_axis=1, concat_axis=2, tiled=True)]
    ppermute x0 -> x44, starting transfers between devices: none -> 55.1 us  [the longest x21 43.7 us: along(): lax.ppermute(value, 'narrow', [(i, (i + shift) % narrow) for i in range(n...]
  transfers between devices with their start and end apart: 28 -> 47, of which waited for: 14 -> 22; matrix products, arithmetic and copies ran while one was open for 37% -> 6% of each run, Pallas kernels for 0% -> 5%
where the time goes in v1:
time: 546 us
  waiting for transfers between devices  237 us (43%)
  Pallas kernels  125 us (23%)
  starting transfers between devices  55.2 us (10%)
  blocking collectives  49.9 us (9%)
  local copies, waits for them, and re-layouts  38.6 us (7%)
  between operations  22.4 us (4%)
  other arithmetic  17 us (3%)
    ppermute x21, waiting for transfers between devices, along(): lax.ppermute(value, 'narrow', [(i, (i + shift) % narrow) for i in range(n...  182 us
    pallas_call x1, Pallas kernels, ffn_call(): call(ffn_kernel, (chunks,), 0, [whole, whole, weight_spec], [whole, whole...  58.1 us
    psum x1, blocking collectives, per_device(): gain_sum = lax.psum(gain_line, ('dp', 'narrow'))  49.9 us
    ppermute x21, starting transfers between devices, along(): lax.ppermute(value, 'narrow', [(i, (i + shift) % narrow) for i in range(n...  43.7 us
    ppermute x7, waiting for transfers between devices, to_chip(): return lax.ppermute(value, 'dp', [(i, i ^ 2 * flip) for i in range(dp)])  24.2 us
    reduce_scatter x2, waiting for transfers between devices, reduce_chips(): lax.psum_scatter(flat, 'dp', scatter_dimension=0, tiled=True, axis_index_...  19.6 us
    pallas_call x1, Pallas kernels, attend_back_call(): call(attend_back_kernel, (pairs, blocks), 1, [some, every, every, some, s...  19.2 us
    unnamed x65, local copies, waits for them, and re-layouts  18 us
  transfers between devices with their start and end apart: 47, of which 22 were waited for; matrix products, arithmetic and copies ran while one was open for 6% of the time, Pallas kernels for 5%

profile of v1, /device:TPU:0, one launch (start us, length us, event | category | flops | bytes accessed | tf_op | source)
XLA Modules:
  0.0 545.9 jit_solution(16720732331375128155)
XLA Ops:
  13.7 4.8 collective-permute-start.13
  20.3 6.5 %collective-permute-done.13 = bf16[512,256]{1,0:T(8,128)(2,1)S(1)} collective-permute-done((bf16[512,256]{1,0:T(8,128)(2,1)S(1)}, bf16[512,256]{1,0:T(8,128)(2,1)S(1)}, u32[]{:S(2)}, u32[]{:S(2)}) %collective-permute-start.13) | collective-permute-done | bytes 262176 | tf_op jit(solution)/shard_map/ppermute | solution.py:559
  28.1 24.0 %collective-permute-done.12 = bf16[512,256]{1,0:T(8,128)(2,1)S(1)} collective-permute-done((bf16[512,256]{1,0:T(8,128)(2,1)S(1)}, bf16[512,256]{1,0:T(8,128)(2,1)S(1)}, u32[]{:S(2)}, u32[]{:S(2)}) %collective-permute-start.12) | collective-permute-done | bytes 262176 | tf_op jit(solution)/shard_map/ppermute | solution.py:559
  73.3 4.7 collective-permute-done.3
  78.2 32.0 %collective-permute-done.2 = bf16[144,1024]{1,0:T(8,128)(2,1)S(1)} collective-permute-done((bf16[144,1024]{1,0:T(8,128)(2,1)}, bf16[144,1024]{1,0:T(8,128)(2,1)S(1)}, u32[]{:S(2)}, u32[]{:S(2)}) %collective-permute-start.2) | collective-permute-done | bytes 294944 | tf_op jit(solution)/shard_map/ppermute | solution.py:559
  117.0 22.5 %collective-permute-done.16 = bf16[2,512,256]{2,1,0:T(8,128)(2,1)S(1)} collective-permute-done((bf16[2,512,256]{2,1,0:T(8,128)(2,1)S(1)}, bf16[2,512,256]{2,1,0:T(8,128)(2,1)S(1)}, u32[]{:S(2)}, u32[]{:S(2)}) %collective-permute-start.16) | collective-permute-done | bytes 524320 | tf_op jit(solution)/shard_map/ppermute | solution.py:564
  143.4 5.5 shard_map.203
  150.3 15.3 %shard_map.204 = (bf16[1152,512]{1,0:T(8,128)(2,1)S(1)}, bf16[4,3,1152,768]{3,2,1,0:T(8,128)(2,1)}) custom-call(s32[1]{0:T(128)} %dynamic_slice.201.flag_ref, bf16[1152,512]{1,0:T(8,128)(2,1)S(1)} %get-tuple-element.33.q_ref, bf16[1152,512]{1,0:T(8,128)(2,1)S(1)} %get-tuple-element.34.k_ref, bf16[1152,512]{1,0:T(8,128)(2,1)S(1)} %get-tuple-element.35.v_ref), custom_call_target="tpu_custom_call" | custom-call | flops 10871635968 | bytes 29360128 | tf_op jit(solution)/shard_map/pallas_call | solution.py:133
  168.2 9.1 %collective-permute-start.21 = (bf16[144,1024]{1,0:T(8,128)(2,1)S(1)}, bf16[144,1024]{1,0:T(8,128)(2,1)S(1)}, u32[]{:S(2)}, u32[]{:S(2)}) collective-permute-start(bf16[144,1024]{1,0:T(8,128)(2,1)S(1)} %get-tuple-element.86), channel_id=1, source_target_pairs={{0,2},{1,3},{2,0},{3,1},{4,6},{5,7},{6,4},{7,5},{8,10},{9,11},{10,... | collective-permute-start | bytes 884744 | tf_op jit(solution)/shard_map/ppermute | solution.py:559
  179.3 24.5 %collective-permute-done.21 = bf16[144,1024]{1,0:T(8,128)(2,1)S(1)} collective-permute-done((bf16[144,1024]{1,0:T(8,128)(2,1)S(1)}, bf16[144,1024]{1,0:T(8,128)(2,1)S(1)}, u32[]{:S(2)}, u32[]{:S(2)}) %collective-permute-start.21) | collective-permute-done | bytes 294944 | tf_op jit(solution)/shard_map/ppermute | solution.py:559
  214.4 58.1 %shard_map.207 = (bf16[1152,1024]{1,0:T(8,128)(2,1)}, bf16[1152,1024]{1,0:T(8,128)(2,1)}, bf16[4,4,3,352,256]{4,3,2,1,0:T(8,128)(2,1)}) custom-call(bf16[1152,1024]{1,0:T(8,128)(2,1)} %copy-done.12, bf16[1152,1024]{1,0:T(8,128)(2,1)} %bitcast.188, bf16[4,4,3,352,256]{4,3,2,1,0:T(8,128)(2,1)} %bitcast.261), custom_call_target="tpu_custom_call" | custom-call | flops 29896998912 | bytes 29360128 | tf_op jit(solution)/shard_map/pallas_call | solution.py:278
  272.5 4.6 collective-permute-done.30.two_ref
  280.5 7.3 %shard_map.209 = (f32[1152,1024]{1,0:T(8,128)}, bf16[1152,1024]{1,0:T(8,128)(2,1)S(1)}, bf16[1152,512]{1,0:T(8,128)(2,1)S(1)}, f32[1,1024]{1,0:T(1,128)S(1)}) custom-call(s32[1]{0:T(128)} %bitcast.17.me_ref, f32[1152,1024]{1,0:T(8,128)} %copy-done.1, bf16[1152,1024]{1,0:T(8,128)(2,1)S(1)} %copy-done.9, ...), custom_call_target="tpu_custom_call" | custom-call | flops 1207959552 | bytes 23068672 | tf_op jit(solution)/shard_map/pallas_call | solution.py:327
  288.8 19.2 %shard_map.210 = (bf16[1152,512]{1,0:T(8,128)(2,1)S(1)}, bf16[1152,512]{1,0:T(8,128)(2,1)S(1)}, bf16[1152,512]{1,0:T(8,128)(2,1)S(1)}) custom-call(s32[1]{0:T(128)} %dynamic_slice.201.flag_ref, bf16[1152,512]{1,0:T(8,128)(2,1)S(1)} %copy-done.17, bf16[1152,512]{1,0:T(8,128)(2,1)S(1)} %copy-done.19, bf16[1152,512]{1,0:T(8,128)(2,1)} %copy-done.20, ...), custom_call_target="tpu_custom_call" | custom-call | flops 21743271936 | bytes 31457280 | tf_op jit(solution)/shard_map/pallas_call | solution.py:405
  308.1 14.2 %shard_map.211 = (bf16[1152,1024]{1,0:T(8,128)(2,1)S(1)}, bf16[4,4,512,256]{3,2,1,0:T(8,128)(2,1)}) custom-call(s32[1]{0:T(128)} %bitcast.17.me_ref, bf16[1152,512]{1,0:T(8,128)(2,1)S(1)} %get-tuple-element.44.dq_ref, bf16[1152,512]{1,0:T(8,128)(2,1)S(1)} %get-tuple-element.45.dk_ref, bf16[1152,512]{1,0:T(8,128)(2,1)S(1)} %get-tuple-element.46.dv_ref, ...), custom_call_target="tpu_custom_call" | custom-call | flops 8455716864 | bytes 25165824 | tf_op jit(solution)/shard_map/pallas_call | solution.py:455
  332.6 10.3 %collective-permute-start.27 = (bf16[144,1024]{1,0:T(8,128)(2,1)}, bf16[144,1024]{1,0:T(8,128)(2,1)}, u32[]{:S(2)}, u32[]{:S(2)}) collective-permute-start(bf16[144,1024]{1,0:T(8,128)(2,1)} %get-tuple-element.76), channel_id=1, source_target_pairs={{0,2},{1,3},{2,0},{3,1},{4,6},{5,7},{6,4},{7,5},{8,10},{9,11},{10,... | collective-permute-start | bytes 884744 | tf_op jit(solution)/shard_map/ppermute | solution.py:559
  345.0 24.6 %collective-permute-done.27 = bf16[144,1024]{1,0:T(8,128)(2,1)} collective-permute-done((bf16[144,1024]{1,0:T(8,128)(2,1)}, bf16[144,1024]{1,0:T(8,128)(2,1)}, u32[]{:S(2)}, u32[]{:S(2)}) %collective-permute-start.27) | collective-permute-done | bytes 294944 | tf_op jit(solution)/shard_map/ppermute | solution.py:559
  378.7 49.9 %psum.7 = f32[2,1024]{1,0:T(2,128)S(1)} all-reduce(f32[2,1024]{1,0:T(2,128)S(1)} %pad_maximum_fusion.12), channel_id=1, replica_groups=mesh['dp'=8,'narrow'=4] {'dp','narrow'}, use_global_device_ids=true, to_apply=%region_0.1 | all-reduce | flops 2048 | bytes 16384 | tf_op jit(solution)/shard_map/psum | solution.py:695
  437.9 10.7 %collective-permute-done.36 = bf16[512,256]{1,0:T(8,128)(2,1)S(1)} collective-permute-done((bf16[512,256]{1,0:T(8,128)(2,1)S(1)}, bf16[512,256]{1,0:T(8,128)(2,1)S(1)}, u32[]{:S(2)}, u32[]{:S(2)}) %collective-permute-start.36) | collective-permute-done | bytes 262176 | tf_op jit(solution)/shard_map/ppermute | solution.py:559
  448.6 10.1 %collective-permute-done.37 = bf16[512,256]{1,0:T(8,128)(2,1)S(1)} collective-permute-done((bf16[512,256]{1,0:T(8,128)(2,1)S(1)}, bf16[512,256]{1,0:T(8,128)(2,1)S(1)}, u32[]{:S(2)}, u32[]{:S(2)}) %collective-permute-start.37) | collective-permute-done | bytes 262176 | tf_op jit(solution)/shard_map/ppermute | solution.py:559
  460.5 19.6 %reduce-scatter.5.cloned.1.call-done = bf16[4224,256]{1,0:T(8,128)(2,1)} async-done(((bf16[16896,256]{1,0:T(8,128)(2,1)}), bf16[4224,256]{1,0:T(8,128)(2,1)}) %reduce-scatter.5.cloned.1.call-update) | async-done | bytes 2162704 | tf_op jit(solution)/shard_map/reduce_scatter | solution.py:669
  487.6 11.1 %collective-permute-done.40 = bf16[1056,256]{1,0:T(8,128)(2,1)S(1)} collective-permute-done((bf16[1056,256]{1,0:T(8,128)(2,1)S(1)}, bf16[1056,256]{1,0:T(8,128)(2,1)S(1)}, u32[]{:S(2)}, u32[]{:S(2)}) %collective-permute-start.40) | collective-permute-done | bytes 540704 | tf_op jit(solution)/shard_map/ppermute | solution.py:559
  498.7 9.8 %collective-permute-done.42 = bf16[1056,256]{1,0:T(8,128)(2,1)S(1)} collective-permute-done((bf16[1056,256]{1,0:T(8,128)(2,1)S(1)}, bf16[1056,256]{1,0:T(8,128)(2,1)S(1)}, u32[]{:S(2)}, u32[]{:S(2)}) %collective-permute-start.42) | collective-permute-done | bytes 540704 | tf_op jit(solution)/shard_map/ppermute | solution.py:559
  508.4 23.8 %collective-permute-done.41 = bf16[1056,256]{1,0:T(8,128)(2,1)S(1)} collective-permute-done((bf16[1056,256]{1,0:T(8,128)(2,1)S(1)}, bf16[1056,256]{1,0:T(8,128)(2,1)S(1)}, u32[]{:S(2)}, u32[]{:S(2)}) %collective-permute-start.41) | collective-permute-done | bytes 540704 | tf_op jit(solution)/shard_map/ppermute | solution.py:559
  (230 shorter events, 101.5 us)
Async XLA Ops:
  7.2 207.2 %all-gather.2.cloned.1.call-start = ((), (), s32[]{:S(2)}) async-start(), calls=%async_computation.2 | async-start | bytes 9191424 | tf_op jit(solution)/shard_map/all_gather | solution.py:647
  11.2 421.5 %reduce-scatter.3.cloned.1.call-start = ((), (), s32[]{:S(2)}) async-start(), calls=%async_computation.3 | async-start | bytes 5242880 | tf_op jit(solution)/shard_map/reduce_scatter | solution.py:669
  12.6 45.4 %collective-permute-start = (bf16[2,144,1024]{2,1,0:T(8,128)(2,1)S(1)}, bf16[2,144,1024]{2,1,0:T(8,128)(2,1)S(1)}, u32[]{:S(2)}, u32[]{:S(2)}) collective-permute-start(bf16[2,144,1024]{2,1,0:T(8,128)(2,1)S(1)} %get-tuple-element.101), channel_id=1, source_target_pairs={{0,4},{4,0},{8,12},{12,8},{16,20},{20,16},{24,28},{28,24},{1,5},{5... | collective-permute-start | bytes 1769480 | tf_op jit(solution)/shard_map/ppermute | solution.py:556
  18.5 33.6 %collective-permute-start.12 = (bf16[512,256]{1,0:T(8,128)(2,1)S(1)}, bf16[512,256]{1,0:T(8,128)(2,1)S(1)}, u32[]{:S(2)}, u32[]{:S(2)}) collective-permute-start(bf16[512,256]{1,0:T(8,128)(2,1)S(1)} %maximum_select_fusion.10), channel_id=1, source_target_pairs={{0,2},{1,3},{2,0},{3,1},{4,6},{5,7},{6,4},{7,5},{8,10},{9,11},{10,... | collective-permute-start | bytes 786440 | tf_op jit(solution)/shard_map/ppermute | solution.py:559
  18.5 33.6 %collective-permute-start.11 = (bf16[512,256]{1,0:T(8,128)(2,1)S(1)}, bf16[512,256]{1,0:T(8,128)(2,1)S(1)}, u32[]{:S(2)}, u32[]{:S(2)}) collective-permute-start(bf16[512,256]{1,0:T(8,128)(2,1)S(1)} %maximum_select_fusion.10), channel_id=1, source_target_pairs={{0,1},{1,2},{2,3},{3,0},{4,5},{5,6},{6,7},{7,4},{8,9},{9,10},{10,1... | collective-permute-start | bytes 786440 | tf_op jit(solution)/shard_map/ppermute | solution.py:559
  20.1 38.9 %collective-permute-start.5 = (f32[2]{0:T(128)S(1)}, f32[2]{0:T(128)S(1)}, u32[]{:S(2)}, u32[]{:S(2)}) collective-permute-start(f32[2]{0:T(128)S(1)} %convert_element_type.65), channel_id=1, source_target_pairs={{0,4},{4,0},{8,12},{12,8},{16,20},{20,16},{24,28},{28,24},{1,5},{5... | collective-permute-start | bytes 32 | tf_op jit(solution)/shard_map/ppermute | solution.py:652
  26.8 35.9 %collective-permute-start.7 = (bf16[2,256]{1,0:T(2,128)(2,1)S(1)}, bf16[2,256]{1,0:T(2,128)(2,1)S(1)}, u32[]{:S(2)}, u32[]{:S(2)}) collective-permute-start(bf16[2,256]{1,0:T(2,128)(2,1)S(1)} %broadcast_select_fusion), channel_id=1, source_target_pairs={{0,8},{4,12},{8,0},{12,4},{16,24},{20,28},{24,16},{28,20},{1,9},{5... | collective-permute-start | bytes 3080 | tf_op jit(solution)/shard_map/ppermute | solution.py:564
  54.9 57.1 %collective-permute-start.14 = (bf16[4,512,256]{2,1,0:T(8,128)(2,1)}, bf16[4,512,256]{2,1,0:T(8,128)(2,1)}, u32[]{:S(2)}, u32[]{:S(2)}) collective-permute-start(bf16[4,512,256]{2,1,0:T(8,128)(2,1)} %get-tuple-element.109), channel_id=1, source_target_pairs={{0,8},{4,12},{8,0},{12,4},{16,24},{20,28},{24,16},{28,20},{1,9},{5... | collective-permute-start | bytes 3145736 | tf_op jit(solution)/shard_map/ppermute | solution.py:564
  56.4 57.4 %collective-permute-start.15 = (bf16[4,512,256]{2,1,0:T(8,128)(2,1)}, bf16[4,512,256]{2,1,0:T(8,128)(2,1)}, u32[]{:S(2)}, u32[]{:S(2)}) collective-permute-start(bf16[4,512,256]{2,1,0:T(8,128)(2,1)} %get-tuple-element.109), channel_id=1, source_target_pairs={{0,16},{4,20},{8,24},{12,28},{16,0},{20,4},{24,8},{28,12},{1,17},{... | collective-permute-start | bytes 3145736 | tf_op jit(solution)/shard_map/ppermute | solution.py:564
  59.1 51.0 %collective-permute-start.2 = (bf16[144,1024]{1,0:T(8,128)(2,1)}, bf16[144,1024]{1,0:T(8,128)(2,1)S(1)}, u32[]{:S(2)}, u32[]{:S(2)}) collective-permute-start(bf16[144,1024]{1,0:T(8,128)(2,1)} %get-tuple-element.98), channel_id=1, source_target_pairs={{0,2},{1,3},{2,0},{3,1},{4,6},{5,7},{6,4},{7,5},{8,10},{9,11},{10,... | collective-permute-start | bytes 884744 | tf_op jit(solution)/shard_map/ppermute | solution.py:559
  62.7 48.7 %collective-permute-start.1 = (bf16[144,1024]{1,0:T(8,128)(2,1)}, bf16[144,1024]{1,0:T(8,128)(2,1)S(1)}, u32[]{:S(2)}, u32[]{:S(2)}) collective-permute-start(bf16[144,1024]{1,0:T(8,128)(2,1)} %get-tuple-element.99), channel_id=1, source_target_pairs={{0,1},{1,2},{2,3},{3,0},{4,5},{5,6},{6,7},{7,4},{8,9},{9,10},{10,1... | collective-permute-start | bytes 884744 | tf_op jit(solution)/shard_map/ppermute | solution.py:559
  78.0 37.5 %collective-permute-start.8 = (bf16[2,256]{1,0:T(2,128)(2,1)S(1)}, bf16[2,256]{1,0:T(2,128)(2,1)S(1)}, u32[]{:S(2)}, u32[]{:S(2)}) collective-permute-start(bf16[2,256]{1,0:T(2,128)(2,1)S(1)} %broadcast_select_fusion), channel_id=1, source_target_pairs={{0,16},{4,20},{8,24},{12,28},{16,0},{20,4},{24,8},{28,12},{1,17},{... | collective-permute-start | bytes 3080 | tf_op jit(solution)/shard_map/ppermute | solution.py:564
  111.9 31.2 %collective-permute-start.4 = (bf16[4,144,1024]{2,1,0:T(8,128)(2,1)S(1)}, bf16[4,144,1024]{2,1,0:T(8,128)(2,1)S(1)}, u32[]{:S(2)}, u32[]{:S(2)}) collective-permute-start(bf16[4,144,1024]{2,1,0:T(8,128)(2,1)S(1)} %get-tuple-element.91), channel_id=1, source_target_pairs={{0,4},{4,0},{8,12},{12,8},{16,20},{20,16},{24,28},{28,24},{1,5},{5... | collective-permute-start | bytes 3538952 | tf_op jit(solution)/shard_map/ppermute | solution.py:556
  112.0 55.8 %collective-permute-start.19 = (bf16[2,144,1024]{2,1,0:T(8,128)(2,1)S(1)}, bf16[2,144,1024]{2,1,0:T(8,128)(2,1)S(1)}, u32[]{:S(2)}, u32[]{:S(2)}) collective-permute-start(bf16[2,144,1024]{2,1,0:T(8,128)(2,1)S(1)} %get-tuple-element.89), channel_id=1, source_target_pairs={{0,4},{4,0},{8,12},{12,8},{16,20},{20,16},{24,28},{28,24},{1,5},{5... | collective-permute-start | bytes 1769480 | tf_op jit(solution)/shard_map/ppermute | solution.py:556
  167.7 41.5 %collective-permute-start.18 = (bf16[1152,1024]{1,0:T(8,128)(2,1)S(1)}, bf16[1152,1024]{1,0:T(8,128)(2,1)S(1)}, u32[]{:S(2)}, u32[]{:S(2)}) collective-permute-start(bf16[1152,1024]{1,0:T(8,128)(2,1)S(1)} %shard_map.205.one_ref), channel_id=1, source_target_pairs={{0,4},{4,0},{8,12},{12,8},{16,20},{20,16},{24,28},{28,24},{1,5},{5... | collective-permute-start | bytes 7077896 | tf_op jit(solution)/shard_map/ppermute | solution.py:556
  168.2 35.7 %collective-permute-start.21 = (bf16[144,1024]{1,0:T(8,128)(2,1)S(1)}, bf16[144,1024]{1,0:T(8,128)(2,1)S(1)}, u32[]{:S(2)}, u32[]{:S(2)}) collective-permute-start(bf16[144,1024]{1,0:T(8,128)(2,1)S(1)} %get-tuple-element.86), channel_id=1, source_target_pairs={{0,2},{1,3},{2,0},{3,1},{4,6},{5,7},{6,4},{7,5},{8,10},{9,11},{10,... | collective-permute-start | bytes 884744 | tf_op jit(solution)/shard_map/ppermute | solution.py:559
  323.7 156.5 %reduce-scatter.5.cloned.1.call-start = ((), (), s32[]{:S(2)}) async-start(), calls=%async_computation.4 | async-start | bytes 10813440 | tf_op jit(solution)/shard_map/reduce_scatter | solution.py:669
  327.5 44.6 %collective-permute-start.31 = (bf16[4,144,1024]{2,1,0:T(8,128)(2,1)}, bf16[4,144,1024]{2,1,0:T(8,128)(2,1)S(1)}, u32[]{:S(2)}, u32[]{:S(2)}) collective-permute-start(bf16[4,144,1024]{2,1,0:T(8,128)(2,1)} %dynamic-slice_bitcast_fusion), channel_id=1, source_target_pairs={{0,4},{4,0},{8,12},{12,8},{16,20},{20,16},{24,28},{28,24},{1,5},{5... | collective-permute-start | bytes 3538952 | tf_op jit(solution)/shard_map/ppermute | solution.py:556
  332.6 36.9 %collective-permute-start.27 = (bf16[144,1024]{1,0:T(8,128)(2,1)}, bf16[144,1024]{1,0:T(8,128)(2,1)}, u32[]{:S(2)}, u32[]{:S(2)}) collective-permute-start(bf16[144,1024]{1,0:T(8,128)(2,1)} %get-tuple-element.76), channel_id=1, source_target_pairs={{0,2},{1,3},{2,0},{3,1},{4,6},{5,7},{6,4},{7,5},{8,10},{9,11},{10,... | collective-permute-start | bytes 884744 | tf_op jit(solution)/shard_map/ppermute | solution.py:559
  376.6 52.0 %collective-permute-start.34 = (bf16[144,1024]{1,0:T(8,128)(2,1)S(1)}, bf16[144,1024]{1,0:T(8,128)(2,1)S(1)}, u32[]{:S(2)}, u32[]{:S(2)}) collective-permute-start(bf16[144,1024]{1,0:T(8,128)(2,1)S(1)} %get-tuple-element.65), channel_id=1, source_target_pairs={{0,3},{1,0},{2,1},{3,2},{4,7},{5,4},{6,5},{7,6},{8,11},{9,8},{10,9... | collective-permute-start | bytes 884744 | tf_op jit(solution)/shard_map/ppermute | solution.py:559
  376.7 52.0 %collective-permute-start.33 = (bf16[144,1024]{1,0:T(8,128)(2,1)S(1)}, bf16[144,1024]{1,0:T(8,128)(2,1)S(1)}, u32[]{:S(2)}, u32[]{:S(2)}) collective-permute-start(bf16[144,1024]{1,0:T(8,128)(2,1)S(1)} %get-tuple-element.66), channel_id=1, source_target_pairs={{0,2},{1,3},{2,0},{3,1},{4,6},{5,7},{6,4},{7,5},{8,10},{9,11},{10,... | collective-permute-start | bytes 884744 | tf_op jit(solution)/shard_map/ppermute | solution.py:559
  376.8 51.9 %collective-permute-start.32 = (bf16[144,1024]{1,0:T(8,128)(2,1)S(1)}, bf16[144,1024]{1,0:T(8,128)(2,1)S(1)}, u32[]{:S(2)}, u32[]{:S(2)}) collective-permute-start(bf16[144,1024]{1,0:T(8,128)(2,1)S(1)} %get-tuple-element.67), channel_id=1, source_target_pairs={{0,1},{1,2},{2,3},{3,0},{4,5},{5,6},{6,7},{7,4},{8,9},{9,10},{10,1... | collective-permute-start | bytes 884744 | tf_op jit(solution)/shard_map/ppermute | solution.py:559
  431.3 54.9 %collective-permute-start.29 = (bf16[2,144,1024]{2,1,0:T(8,128)(2,1)S(1)}, bf16[2,144,1024]{2,1,0:T(8,128)(2,1)S(1)}, u32[]{:S(2)}, u32[]{:S(2)}) collective-permute-start(bf16[2,144,1024]{2,1,0:T(8,128)(2,1)S(1)} %get-tuple-element.69), channel_id=1, source_target_pairs={{0,4},{4,0},{8,12},{12,8},{16,20},{20,16},{24,28},{28,24},{1,5},{5... | collective-permute-start | bytes 1769480 | tf_op jit(solution)/shard_map/ppermute | solution.py:556
  485.5 46.7 %collective-permute-start.41 = (bf16[1056,256]{1,0:T(8,128)(2,1)S(1)}, bf16[1056,256]{1,0:T(8,128)(2,1)S(1)}, u32[]{:S(2)}, u32[]{:S(2)}) collective-permute-start(bf16[1056,256]{1,0:T(8,128)(2,1)S(1)} %get-tuple-element.57), channel_id=1, source_target_pairs={{0,2},{1,3},{2,0},{3,1},{4,6},{5,7},{6,4},{7,5},{8,10},{9,11},{10,... | collective-permute-start | bytes 1622024 | tf_op jit(solution)/shard_map/ppermute | solution.py:559
  (55 other events, 482.7 us)
Sparse Core Ops, SparseCore 0:
  11.4 166.1 all-gather.1
  323.8 63.5 reduce-scatter.2
  390.8 89.2 reduce-scatter.4
